TPU v7x, 512 devices: a whole 4x8x8 slice. The times are simulated.
512 devices in a mesh: mode: 32 (over x, y), orb: 16 (over z, core).
Axes of the slice: x: 4, y: 8, z: 8, core: 2. Of those that a mesh axis runs over, the one named last changes fastest.
Arguments:
- correlators: float32 [512, 2, 256, 256], P('mode', None, 'orb'), may hold values from -6 to 6
- density: float32 [2, 256, 256], P(None, 'orb'), may hold values from -6 to 6
- bare_hamiltonian: float32 [2, 256, 256], P(None, 'orb'), may hold values from -0.375 to 0.375
- coupling: float32 [512], P('mode'), may hold values from -0.25 to 0.25
- propagator: float32 [512, 512], P('mode'), may hold values from -0.25 to 0.25
Outputs:
- correlators_out: float32 [512, 2, 256, 256], P('mode', None, 'orb')
- density_out: float32 [2, 256, 256], P(None, 'orb')
All inputs are finite; a program needn't handle non-finite values.
Results may differ from a plain program's by a relative error of at most 0.0001.
Values sent between devices are 32-bit elements; how exact they have to be, the bound alone decides.
A program may use at most 64 MiB of HBM per device.

v0:
```python
import jax
import jax.numpy as jnp
from jax import lax
from jax.sharding import PartitionSpec as P

time_step = 0.1
field_weight = 0.0625


def contract(form, first, second):
    return jnp.einsum(form, first, second, precision=lax.Precision.HIGHEST)


def right_product(stack, matrix):
    real = contract("mij,jk->mik", stack[:, 0], matrix[0]) - contract(
        "mij,jk->mik", stack[:, 1], matrix[1]
    )
    imag = contract("mij,jk->mik", stack[:, 0], matrix[1]) + contract(
        "mij,jk->mik", stack[:, 1], matrix[0]
    )
    return jnp.stack([real, imag], axis=1)


def advance(stack, commut, weights, dens):
    turned = jnp.stack([commut[:, 1], -commut[:, 0]], axis=1)
    return stack + time_step * turned + time_step * weights[:, None, None, None] * dens[None]


def gather_hamil(rows):
    return lax.all_gather(rows, "orb", axis=1, tiled=True)


def rows_substep(stacks, dens_rows, hamil, coupling):
    items, parts, row_count, width = stacks.shape
    blocks = lax.axis_size("orb")
    col_count = width // blocks
    right = right_product(stacks, hamil)
    outgoing = stacks.reshape(items, parts, row_count, blocks, col_count)
    outgoing = outgoing.transpose(0, 1, 3, 4, 2).reshape(
        items, parts, blocks, col_count * row_count
    )
    received = lax.all_to_all(outgoing, "orb", split_axis=2, concat_axis=2, tiled=True)
    count = received.shape[0]
    columns = received.reshape(count, parts, blocks, col_count, row_count)
    columns = columns.transpose(0, 1, 3, 2, 4).reshape(count, parts, col_count, width)
    real = contract("mcj,ij->mci", columns[:, 0], hamil[0]) - contract(
        "mcj,ij->mci", columns[:, 1], hamil[1]
    )
    imag = contract("mcj,ij->mci", columns[:, 0], hamil[1]) + contract(
        "mcj,ij->mci", columns[:, 1], hamil[0]
    )
    product = jnp.stack([real, imag], axis=1).reshape(count, parts, col_count, blocks, row_count)
    product = product.transpose(0, 1, 3, 2, 4).reshape(count, parts, blocks, col_count * row_count)
    returned = lax.all_to_all(product, "orb", split_axis=2, concat_axis=2, tiled=True)
    returned = returned.reshape(count, parts, blocks, col_count, row_count)
    left = returned.transpose(0, 1, 4, 2, 3).reshape(count, parts, row_count, width)
    updated = advance(stacks, left - right, coupling, dens_rows)
    partial_value = contract("m,mcrk->crk", coupling, updated)
    collision = lax.psum(partial_value, "mode")
    return (updated, dens_rows + time_step * collision)


def propagate(stacks, propagator):
    local_modes = stacks.shape[0]
    groups = lax.axis_size("mode")
    flat = stacks.reshape(local_modes, groups, -1)
    spread = lax.all_to_all(flat, "mode", split_axis=1, concat_axis=0, tiled=True)
    entries = spread[:, 0, :]
    mixed = contract("mn,nx->mx", lax.all_gather(propagator, "mode", axis=0, tiled=True), entries)
    returned = lax.all_to_all(mixed[:, None, :], "mode", split_axis=0, concat_axis=1, tiled=True)
    return returned.reshape(stacks.shape)


def on_device(correlators, density, bare_hamiltonian, coupling, propagator):
    dens_rows = density
    hamil = gather_hamil(bare_hamiltonian + field_weight * density)
    stacks = correlators
    for turn in range(2):
        stacks, dens_rows = rows_substep(stacks, dens_rows, hamil, coupling)
        hamil = gather_hamil(bare_hamiltonian + field_weight * dens_rows)
    stacks = propagate(stacks, propagator)
    stacks, dens_rows = rows_substep(stacks, dens_rows, hamil, coupling)
    return (stacks, dens_rows)


def solution(mesh):
    in_specs = (
        P("mode", None, "orb", None),
        P(None, "orb", None),
        P(None, "orb", None),
        P("mode"),
        P("mode", None),
    )
    out_specs = (P("mode", None, "orb", None), P(None, "orb", None))
    return jax.shard_map(
        on_device, mesh=mesh, in_specs=in_specs, out_specs=out_specs, check_vma=False
    )
```

profile of v0, /device:TPU:192, one launch (start us, length us, event | category | flops | bytes accessed | tf_op | source)
XLA Modules:
  0.0 805.0 jit_solution(5045939652481662568)
XLA Ops:
  15.4 8.2 %all-to-all-start = ((f32[16,2,16,256]{3,1,0,2:T(2,128)}), f32[16,2,16,256]{3,1,0,2:T(2,128)S(1)}, u32[]{:S(2)}, u32[]{:S(2)}) async-start(f32[16,2,16,256]{3,1,0,2:T(2,128)} %copy.38), calls=%async_computation | async-start | bytes 1048576 | tf_op jit(solution)/shard_map/all_to_all | solution.py:42
  23.6 24.9 %all_gather.12 = f32[2,256,256]{2,1,0:T(8,128)S(1)} all-gather(f32[2,16,256]{2,1,0:T(8,128)S(1)} %multiply_add_fusion.5), channel_id=1, replica_groups=mesh['mode'=32,'orb'=16] {'orb'}, dimensions={1}, use_global_device_ids=true | all-gather | bytes 557056 | tf_op jit(solution)/shard_map/all_gather | solution.py:30
  51.4 5.9 copy.40
  73.1 3.5 reshape.97
  77.9 8.8 %all-to-all-start.1 = ((f32[16,2,16,256]{3,1,0,2:T(2,128)}), f32[16,2,16,256]{3,1,0,2:T(2,128)S(1)}, u32[]{:S(2)}, u32[]{:S(2)}) async-start(f32[16,2,16,256]{3,1,0,2:T(2,128)} %copy.43), calls=%async_computation.1 | async-start | bytes 1048576 | tf_op jit(solution)/shard_map/all_to_all | solution.py:54
  88.4 13.4 %all-to-all-done.1 = f32[16,2,16,256]{3,1,0,2:T(2,128)S(1)} async-done(((f32[16,2,16,256]{3,1,0,2:T(2,128)}), f32[16,2,16,256]{3,1,0,2:T(2,128)S(1)}, u32[]{:S(2)}, u32[]{:S(2)}) %all-to-all-start.1) | async-done | bytes 524320 | tf_op jit(solution)/shard_map/all_to_all | solution.py:54
  115.0 5.2 all-to-all-start.2
  120.9 143.3 %psum.21 = f32[2,16,256]{2,1,0:T(8,128)S(1)} all-reduce(f32[2,16,256]{2,1,0:T(8,128)S(1)} %bitcast.232), channel_id=1, replica_groups=mesh['mode'=32,'orb'=16] {'mode'}, use_global_device_ids=true, to_apply=%region_0.0 | all-reduce | flops 8192 | bytes 65536 | tf_op jit(solution)/shard_map/psum | solution.py:59
  264.2 17.0 %all_gather.13 = f32[2,256,256]{2,1,0:T(8,128)S(1)} all-gather(f32[2,16,256]{2,1,0:T(8,128)S(1)} %get-tuple-element.10), channel_id=1, replica_groups=mesh['mode'=32,'orb'=16] {'orb'}, dimensions={1}, use_global_device_ids=true | all-gather | bytes 557056 | tf_op jit(solution)/shard_map/all_gather | solution.py:30
  284.2 5.9 copy.52
  296.8 3.6 copy.53
  312.2 6.3 all-to-all-start.3
  321.5 12.0 %all-to-all-done.3 = f32[16,2,16,256]{3,1,0,2:T(2,128)S(1)} async-done(((f32[16,2,16,256]{3,1,0,2:T(2,128)}), f32[16,2,16,256]{3,1,0,2:T(2,128)S(1)}, u32[]{:S(2)}, u32[]{:S(2)}) %all-to-all-start.3) | async-done | bytes 524320 | tf_op jit(solution)/shard_map/all_to_all | solution.py:54
  340.7 3.9 all-to-all-start.4
  344.6 54.4 %all-gather.2.cloned.1.call-done = f32[512,512]{1,0:T(8,128)} async-done(((f32[16,512]{1,0:T(8,128)}), f32[512,512]{1,0:T(8,128)}) %all-gather.2.cloned.1.call-update) | async-done | bytes 1048592 | tf_op jit(solution)/shard_map/all_gather | solution.py:69
  402.5 19.9 %all_to_all.60 = f32[512,1,256]{2,1,0:T(1,128)S(1)} all-to-all(f32[512,1,256]{2,1,0:T(1,128)S(1)} %copy.60), channel_id=1, replica_groups=mesh['mode'=32,'orb'=16] {'mode'}, dimensions={0} | all-to-all | bytes 1048576 | tf_op jit(solution)/shard_map/all_to_all | solution.py:70
  425.0 5.9 copy.62
  435.6 7.4 all-to-all-start.6
  443.7 139.6 %psum.22 = f32[2,16,256]{2,1,0:T(8,128)S(1)} all-reduce(f32[2,16,256]{2,1,0:T(8,128)S(1)} %bitcast.233), channel_id=1, replica_groups=mesh['mode'=32,'orb'=16] {'mode'}, use_global_device_ids=true, to_apply=%region_1.0 | all-reduce | flops 8192 | bytes 65536 | tf_op jit(solution)/shard_map/psum | solution.py:59
  583.4 17.2 %all_gather.15 = f32[2,256,256]{2,1,0:T(8,128)S(1)} all-gather(f32[2,16,256]{2,1,0:T(8,128)S(1)} %get-tuple-element.8), channel_id=1, replica_groups=mesh['mode'=32,'orb'=16] {'orb'}, dimensions={1}, use_global_device_ids=true | all-gather | bytes 557056 | tf_op jit(solution)/shard_map/all_gather | solution.py:30
  603.5 5.9 copy.65
  630.0 6.7 all-to-all-start.7
  638.5 13.1 %all-to-all-done.7 = f32[16,2,16,256]{3,1,0,2:T(2,128)S(1)} async-done(((f32[16,2,16,256]{3,1,0,2:T(2,128)}), f32[16,2,16,256]{3,1,0,2:T(2,128)S(1)}, u32[]{:S(2)}, u32[]{:S(2)}) %all-to-all-start.7) | async-done | bytes 524320 | tf_op jit(solution)/shard_map/all_to_all | solution.py:54
  659.4 137.7 %psum.23 = f32[2,16,256]{2,1,0:T(8,128)S(1)} all-reduce(f32[2,16,256]{2,1,0:T(8,128)S(1)} %bitcast.234), channel_id=1, replica_groups=mesh['mode'=32,'orb'=16] {'mode'}, use_global_device_ids=true, to_apply=%region_2.0 | all-reduce | flops 8192 | bytes 65536 | tf_op jit(solution)/shard_map/psum | solution.py:59
  (123 shorter events, 120.2 us)
Async XLA Ops:
  10.7 12.9 %copy-start.7 = (f32[2,16,256]{2,1,0:T(8,128)S(1)}, f32[2,16,256]{2,1,0:T(8,128)}, u32[]{:S(2)}) copy-start(f32[2,16,256]{2,1,0:T(8,128)} %param.6) | copy-start | bytes 98308
  10.7 12.9 %copy-start.8 = (f32[2,16,256]{2,1,0:T(8,128)S(1)}, f32[2,16,256]{2,1,0:T(8,128)}, u32[]{:S(2)}) copy-start(f32[2,16,256]{2,1,0:T(8,128)} %param.7) | copy-start | bytes 98308
  15.4 33.1 %all-to-all-start = ((f32[16,2,16,256]{3,1,0,2:T(2,128)}), f32[16,2,16,256]{3,1,0,2:T(2,128)S(1)}, u32[]{:S(2)}, u32[]{:S(2)}) async-start(f32[16,2,16,256]{3,1,0,2:T(2,128)} %copy.38), calls=%async_computation | async-start | bytes 1048576 | tf_op jit(solution)/shard_map/all_to_all | solution.py:42
  69.2 1.6 copy-start.1
  73.1 13.6 %copy-start = (f32[16,2,16,256]{3,2,1,0:T(8,128)S(1)}, f32[16,2,16,256]{3,2,1,0:T(8,128)}, u32[]{:S(2)}) copy-start(f32[16,2,16,256]{3,2,1,0:T(8,128)} %param.5) | copy-start | bytes 1572868
  76.7 11.6 %copy-start.9 = (f32[16]{0:T(128)S(1)}, f32[16]{0:T(128)}, u32[]{:S(2)}) copy-start(f32[16]{0:T(128)} %param.8) | copy-start | bytes 196
  77.9 23.8 %all-to-all-start.1 = ((f32[16,2,16,256]{3,1,0,2:T(2,128)}), f32[16,2,16,256]{3,1,0,2:T(2,128)S(1)}, u32[]{:S(2)}, u32[]{:S(2)}) async-start(f32[16,2,16,256]{3,1,0,2:T(2,128)} %copy.43), calls=%async_computation.1 | async-start | bytes 1048576 | tf_op jit(solution)/shard_map/all_to_all | solution.py:54
  115.0 166.3 %all-to-all-start.2 = ((f32[16,2,16,256]{3,1,0,2:T(2,128)}), f32[16,2,16,256]{3,1,0,2:T(2,128)S(1)}, u32[]{:S(2)}, u32[]{:S(2)}) async-start(f32[16,2,16,256]{3,1,0,2:T(2,128)} %copy.50), calls=%async_computation.2 | async-start | bytes 1048576 | tf_op jit(solution)/shard_map/all_to_all | solution.py:42
  302.8 2.4 copy-start.2
  312.2 21.3 %all-to-all-start.3 = ((f32[16,2,16,256]{3,1,0,2:T(2,128)}), f32[16,2,16,256]{3,1,0,2:T(2,128)S(1)}, u32[]{:S(2)}, u32[]{:S(2)}) async-start(f32[16,2,16,256]{3,1,0,2:T(2,128)} %copy.55), calls=%async_computation.3 | async-start | bytes 1048576 | tf_op jit(solution)/shard_map/all_to_all | solution.py:54
  318.5 80.5 %all-gather.2.cloned.1.call-start = ((), (), s32[]{:S(2)}) async-start(), calls=%async_computation.8 | async-start | bytes 1081344 | tf_op jit(solution)/shard_map/all_gather | solution.py:69
  333.8 5.4 copy-start.6
  340.7 58.3 %all-to-all-start.4 = ((f32[16,32,256]{2,0,1:T(8,128)}), f32[16,32,256]{2,0,1:T(8,128)S(1)}, u32[]{:S(2)}, u32[]{:S(2)}) async-start(f32[16,32,256]{2,0,1:T(8,128)} %copy.59), calls=%async_computation.4 | async-start | bytes 1048576 | tf_op jit(solution)/shard_map/all_to_all | solution.py:67
  435.6 165.0 %all-to-all-start.6 = ((f32[16,2,16,256]{3,1,0,2:T(2,128)}), f32[16,2,16,256]{3,1,0,2:T(2,128)S(1)}, u32[]{:S(2)}, u32[]{:S(2)}) async-start(f32[16,2,16,256]{3,1,0,2:T(2,128)} %copy.63), calls=%async_computation.6 | async-start | bytes 1048576 | tf_op jit(solution)/shard_map/all_to_all | solution.py:42
  613.0 0.9 copy-start.4
  616.6 2.0 copy-start.5
  621.4 1.6 copy-start.3
  630.0 21.6 %all-to-all-start.7 = ((f32[16,2,16,256]{3,1,0,2:T(2,128)}), f32[16,2,16,256]{3,1,0,2:T(2,128)S(1)}, u32[]{:S(2)}, u32[]{:S(2)}) async-start(f32[16,2,16,256]{3,1,0,2:T(2,128)} %copy.68), calls=%async_computation.7 | async-start | bytes 1048576 | tf_op jit(solution)/shard_map/all_to_all | solution.py:54
Sparse Core Ops, SparseCore 0:
  322.5 76.4 all-gather.1
where the time goes:
time: 816 us; the launch traced here: 805 us
  blocking collectives  500 us (61%)
  local copies, waits for them, and re-layouts  123 us (15%)
  waiting for transfers between devices  93.4 us (11%)
  starting transfers between devices  46.7 us (6%)
  matrix products  18.3 us (2%)
  between operations  15.1 us (2%)
  other arithmetic  8.6 us (1%)
    psum x3, blocking collectives, rows_substep(): collision = lax.psum(partial_value, 'mode')  421 us
    all_gather x3, blocking collectives, gather_hamil(): return lax.all_gather(rows, 'orb', axis=1, tiled=True)  59.2 us
    all_gather x1, waiting for transfers between devices, propagate(): lax.all_gather(propagator, 'mode', axis=0, tiled=True)  54.4 us
    all_to_all x3, waiting for transfers between devices, rows_substep(): lax.all_to_all(product, 'orb', split_axis=2, concat_axis=2, tiled=True)  38.5 us
    another operation x12, local copies, waits for them, and re-layouts, rows_substep(): jnp.stack([real, imag], axis=1)  21.9 us
    all_to_all x3, starting transfers between devices, rows_substep(): lax.all_to_all(product, 'orb', split_axis=2, concat_axis=2, tiled=True)  21.8 us
    all_to_all x3, starting transfers between devices, rows_substep(): lax.all_to_all(outgoing, 'orb', split_axis=2, concat_axis=2, tiled=True)  20.8 us
    all_to_all x1, blocking collectives, propagate(): lax.all_to_all(mixed[:, None, :], 'mode', split_axis=0, concat_axis=1, ti...  19.9 us
  transfers between devices with their start and end apart: 8, of which 4 were waited for; matrix products, arithmetic and copies ran while one was open for 2% of the time, Pallas kernels for 0%

commit v1 on v0

v1 whole, which is shorter than its diff:
```python
import functools

import jax
import jax.numpy as jnp
from jax import lax
from jax.experimental import pallas as pl
from jax.experimental.pallas import tpu as pltpu
from jax.sharding import PartitionSpec as P

MESH = pl.DeviceIdType.MESH
time_step = 0.1
field_weight = 0.0625
LANES = 128
CORES = 2
F32 = jnp.float32
BF16 = jnp.bfloat16


def split(value):
    high = value.astype(BF16)
    return high, (value - high.astype(F32)).astype(BF16)


def dot(first, second):
    return jnp.dot(first, second, preferred_element_type=F32)


def dot3(first, second):
    return dot(first[0], second[0]) + (dot(first[0], second[1]) + dot(first[1], second[0]))


def wait_for(ref, sem):
    pltpu.make_async_copy(ref, ref, sem).wait()


def kernel(
    dims,
    gin, dens, bare, coup, prop,
    out, dout,
    stage, got, abuf, ah, al, hb, zbuf, sd, mixed, back, stage2, whole, final, summed, hl, hr,
    send, recv,
):
    nx, ny, nz, rows, size = dims
    nmode, norb = nx * ny, nz * CORES
    modes = nmode * norb
    half = norb // 2
    mu, om = lax.axis_index("mode"), lax.axis_index("orb")
    px, py = mu // ny, mu % ny
    pz, core = om // CORES, om % CORES
    other = 1 - core
    pair = pz * CORES + other

    def push(src, dst, index, target):
        pltpu.make_async_remote_copy(
            src_ref=src, dst_ref=dst, send_sem=send.at[index], recv_sem=recv.at[index],
            device_id=target, device_id_type=MESH,
        ).start()

    def each(count, body):
        def step(k, carry):
            body(k)
            return carry
        lax.fori_loop(1, count, step, 0)

    barrier = pltpu.get_barrier_semaphore()

    def greet_mode(k):
        pl.semaphore_signal(barrier, inc=1, device_id=((mu + k) % nmode, om), device_id_type=MESH)

    def greet_orb(k):
        pl.semaphore_signal(barrier, inc=1, device_id=(mu, (om + k) % norb), device_id_type=MESH)

    each(nmode, greet_mode)
    each(norb, greet_orb)

    abuf[core, mu, :, :modes] = prop[pl.ds(pl.multiple_of(core * half, half), half), :]
    lines = lax.broadcasted_iota(jnp.int32, (half, LANES), 0)
    tile = jnp.zeros((half, LANES), F32)
    for j in range(half):
        tile = jnp.where(lines == j, coup[core * half + j], tile)
    abuf[core, mu, :, modes:] = tile
    for part in range(2):
        hb[part, pz, core] = bare[part] + field_weight * dens[part]
        hb[2 + part, pz, core] = dens[part]

    pl.semaphore_wait(barrier, nmode + norb - 2)

    def send_prop_y(k):
        push(abuf.at[core, mu], abuf.at[core, mu], 0, (px * ny + (py + k) % ny, om))

    each(ny, send_prop_y)

    stage[...] = jnp.swapaxes(gin[...], 0, 1)

    def send_entries(k):
        nu = (mu + k) % nmode
        push(stage.at[nu], got.at[mu], 3, (nu, om))

    each(nmode, send_entries)

    def send_fields(k):
        target = (pz + k) % nz
        push(hb.at[:, pz, core], hb.at[:, pz, core], 4, (mu, target * CORES + core))

    each(nz, send_fields)
    got[mu] = stage[mu]

    wait_for(abuf.at[0, pl.ds(0, ny - 1)], recv.at[0])
    group = pl.ds(pl.multiple_of(px * ny, ny), ny)

    def send_prop_x(k):
        push(abuf.at[core, group], abuf.at[core, group], 1, ((px + k) % nx * ny + py, om))

    each(nx, send_prop_x)
    wait_for(abuf.at[0, pl.ds(0, (nx - 1) * ny)], recv.at[1])
    push(abuf.at[core], abuf.at[core], 2, (mu, pair))
    wait_for(hb.at[:, pl.ds(0, nz - 1), 0], recv.at[4])
    push(hb.at[:, :, core], hb.at[:, :, core], 5, (mu, pair))

    def matrix(part):
        return hb[part].reshape(size, size)

    def store_h(step, real, imag):
        rh, rl = split(time_step * real)
        ih, il = split(time_step * imag)
        for level, (r, i) in enumerate(((rh, ih), (rl, il))):
            hl[step, level, :size, :size] = r
            hl[step, level, size:, size:] = r
            hl[step, level, :size, size:] = -i
            hl[step, level, size:, :size] = i
            hr[step, level, :size, :size] = r
            hr[step, level, size:, size:] = r
            hr[step, level, :size, size:] = i
            hr[step, level, size:, :size] = -i

    def turn(step, real, imag):
        rh, rl = split(real)
        ih, il = split(imag)
        left = dot3(
            (hl[step, 0], hl[step, 1]),
            (jnp.concatenate([rh, ih], 0), jnp.concatenate([rl, il], 0)),
        )
        right = dot3(
            (jnp.concatenate([rh, ih], 1), jnp.concatenate([rl, il], 1)),
            (hr[step, 0], hr[step, 1]),
        )
        return (
            real + (left[size:] - right[:, size:]),
            imag - (left[:size] - right[:, :size]),
        )

    wait_for(hb.at[:, :, 0], recv.at[5])
    store_h(0, matrix(0), matrix(1))

    wait_for(abuf.at[0], recv.at[2])

    def unpack(k, carry):
        block = jnp.concatenate([abuf[0, k, :, :modes], abuf[1, k, :, :modes]], 0)
        high, low = split(block)
        where = pl.ds(pl.multiple_of(k * norb, norb), norb)
        ah[where, :] = high
        al[where, :] = low
        return carry

    lax.fori_loop(0, nmode, unpack, 0)
    weights = jnp.concatenate(
        [abuf[0, :, :, modes:][:, None], abuf[1, :, :, modes:][:, None]], 1
    ).reshape(modes, LANES)
    own = prop[pl.ds(om, 1), :]

    wait_for(got.at[pl.ds(0, nmode - 1)], recv.at[3])
    entries = got[...].reshape(modes, size)
    wide = jnp.concatenate([weights] * (-(-size // LANES)), 1)[:, :size]
    s_row = jnp.sum(wide * entries, axis=0, keepdims=True)
    mixed[...] = dot3((ah[...], al[...]), split(entries))
    d_row = jnp.sum(wide * mixed[...], axis=0, keepdims=True)
    zbuf[pz] = jnp.concatenate([s_row, d_row, jnp.zeros((6, size), F32)], 0)

    def send_sums_z(k):
        push(zbuf.at[pz], zbuf.at[pz], 6, (mu, (pz + k) % nz * CORES + core))

    each(nz, send_sums_z)

    def send_mixed(k):
        nu = (mu + k) % nmode
        push(mixed.at[pl.ds(pl.multiple_of(nu * norb, norb), norb)], back.at[mu], 10, (nu, om))

    each(nmode, send_mixed)
    back[mu] = mixed[pl.ds(pl.multiple_of(mu * norb, norb), norb), :]

    wait_for(zbuf.at[pl.ds(0, nz - 1)], recv.at[6])
    lines = zbuf[...]
    sd[core, mu, 0] = lines[:, 0, :]
    sd[core, mu, 1] = lines[:, 1, :]

    def send_sums_y(k):
        push(sd.at[core, mu], sd.at[core, mu], 7, (px * ny + (py + k) % ny, om))

    each(ny, send_sums_y)

    column = jnp.sum(weights[:, :1] * (ah[...].astype(F32) + al[...].astype(F32)), axis=0, keepdims=True)
    both = jnp.concatenate([own, column, jnp.zeros((6, modes), F32)], 0)
    products = jnp.dot(both, weights, precision=lax.Precision.HIGHEST, preferred_element_type=F32)
    e_own = products[0:1, 0:1]
    f_all = products[1:2, 0:1]
    c_all = jnp.sum(weights * weights, axis=0, keepdims=True)[:, :1]
    c_own = coup[om]

    wait_for(sd.at[0, pl.ds(0, ny - 1)], recv.at[7])

    def send_sums_x(k):
        push(sd.at[core, group], sd.at[core, group], 8, ((px + k) % nx * ny + py, om))

    each(nx, send_sums_x)

    wait_for(back.at[pl.ds(0, nmode - 1)], recv.at[10])
    stage2[...] = jnp.swapaxes(back[...], 0, 1).reshape(norb, 2, rows, size)

    def send_matrix(k):
        target = (om + k) % norb
        push(stage2.at[target], whole.at[:, om], 11, (mu, target))

    each(norb, send_matrix)
    whole[:, om] = stage2[om]

    wait_for(sd.at[0, pl.ds(0, (nx - 1) * ny)], recv.at[8])
    push(sd.at[core], sd.at[core], 9, (mu, pair))
    wait_for(sd.at[0], recv.at[9])
    for side in range(2):
        for part in range(2):
            block = sd[side, part * rows : (part + 1) * rows].reshape(rows, 2 * nz, size)
            block = jnp.swapaxes(block, 0, 1).reshape(2, nz, rows, size)
            summed[0, part, :, side] = block[0]
            summed[1, part, :, side] = block[1]

    def total(which, part):
        return summed[which, part].reshape(size, size)

    dens0 = (matrix(2), matrix(3))
    source = tuple(total(0, part) for part in range(2))
    fields = tuple(matrix(part) for part in range(2))
    densities = [dens0]
    for step in range(2):
        source = turn(step, *source)
        source = tuple(source[p] + (c_all * time_step) * densities[step][p] for p in range(2))
        densities.append(tuple(densities[step][p] + time_step * source[p] for p in range(2)))
        fields = tuple(fields[p] + (field_weight * time_step) * source[p] for p in range(2))
        store_h(step + 1, *fields)

    wait_for(whole.at[:, pl.ds(0, norb - 1)], recv.at[11])
    state = (whole[0].reshape(size, size), whole[1].reshape(size, size))
    for step in range(3):
        weight = e_own if step < 2 else c_own
        state = turn(step, *state)
        state = tuple(state[p] + (weight * time_step) * densities[step][p] for p in range(2))
    for part in range(2):
        final[part] = state[part].reshape(norb, rows, size)

    def send_result(k):
        target = (om + k) % norb
        push(final.at[:, target], out.at[om], 12, (mu, target))

    each(norb, send_result)
    out[om] = final[:, om]

    chain = tuple(total(1, part) for part in range(2))
    for step in range(3):
        weight = f_all if step < 2 else c_all
        chain = turn(step, *chain)
        chain = tuple(chain[p] + (weight * time_step) * densities[step][p] for p in range(2))
    for part in range(2):
        summed[0, part] = (densities[2][part] + time_step * chain[part]).reshape(nz, CORES, rows, size)
    for part in range(2):
        dout[part] = summed[0, part, pz, core]

    wait_for(out.at[pl.ds(0, norb - 1)], recv.at[12])
    wait_for(abuf.at[0, pl.ds(0, ny - 1)], send.at[0])
    wait_for(abuf.at[0, pl.ds(0, (nx - 1) * ny)], send.at[1])
    wait_for(abuf.at[0], send.at[2])
    wait_for(got.at[pl.ds(0, nmode - 1)], send.at[3])
    wait_for(hb.at[:, pl.ds(0, nz - 1), 0], send.at[4])
    wait_for(hb.at[:, :, 0], send.at[5])
    wait_for(zbuf.at[pl.ds(0, nz - 1)], send.at[6])
    wait_for(sd.at[0, pl.ds(0, ny - 1)], send.at[7])
    wait_for(sd.at[0, pl.ds(0, (nx - 1) * ny)], send.at[8])
    wait_for(sd.at[0], send.at[9])
    wait_for(back.at[pl.ds(0, nmode - 1)], send.at[10])
    wait_for(whole.at[:, pl.ds(0, norb - 1)], send.at[11])
    wait_for(out.at[pl.ds(0, norb - 1)], send.at[12])


def build(mesh, nx, ny):
    def on_device(correlators, density, bare_hamiltonian, coupling, propagator):
        local, _, rows, size = correlators.shape
        nmode, norb = mesh.shape["mode"], mesh.shape["orb"]
        nz = norb // CORES
        modes = nmode * norb
        vmem = pl.BlockSpec(memory_space=pltpu.VMEM)
        return pl.pallas_call(
            functools.partial(kernel, (nx, ny, nz, rows, size)),
            out_shape=(
                jax.ShapeDtypeStruct(correlators.shape, F32),
                jax.ShapeDtypeStruct(density.shape, F32),
            ),
            in_specs=[vmem, vmem, vmem, pl.BlockSpec(memory_space=pltpu.SMEM), vmem],
            out_specs=(vmem, vmem),
            scratch_shapes=[
                pltpu.VMEM((nmode, norb, size), F32),
                pltpu.VMEM((nmode, norb, size), F32),
                pltpu.VMEM((2, nmode, norb // 2, modes + LANES), F32),
                pltpu.VMEM((modes, modes), BF16),
                pltpu.VMEM((modes, modes), BF16),
                pltpu.VMEM((4, nz, CORES, rows, size), F32),
                pltpu.VMEM((nz, 8, size), F32),
                pltpu.VMEM((2, nmode, 2, nz, size), F32),
                pltpu.VMEM((modes, size), F32),
                pltpu.VMEM((nmode, norb, size), F32),
                pltpu.VMEM((norb, 2, rows, size), F32),
                pltpu.VMEM((2, norb, rows, size), F32),
                pltpu.VMEM((2, norb, rows, size), F32),
                pltpu.VMEM((2, 2, nz, CORES, rows, size), F32),
                pltpu.VMEM((3, 2, 2 * size, 2 * size), BF16),
                pltpu.VMEM((3, 2, 2 * size, 2 * size), BF16),
                pltpu.SemaphoreType.DMA((13,)),
                pltpu.SemaphoreType.DMA((13,)),
            ],
            compiler_params=pltpu.CompilerParams(
                collective_id=0, has_side_effects=True, vmem_limit_bytes=50 * 1024 * 1024
            ),
        )(
            correlators.reshape(local, 2 * rows, size),
            density, bare_hamiltonian, coupling, propagator,
        )

    in_specs = (
        P("mode", None, "orb", None),
        P(None, "orb", None),
        P(None, "orb", None),
        P("mode"),
        P("mode", None),
    )
    out_specs = (P("mode", None, "orb", None), P(None, "orb", None))
    return jax.shard_map(
        on_device, mesh=mesh, in_specs=in_specs, out_specs=out_specs, check_vma=False
    )


def solution(mesh):
    return build(mesh, 4, mesh.shape["mode"] // 4)
```

time: 816 us -> 92.7 us (0.11)
  the two profiles are of different devices: /device:TPU:192 before, /device:TPU:1 now
where the time goes in v1:
time: 92.7 us; the launch traced here: 92.3 us
  Pallas kernels  86.3 us (93%)
  local copies, waits for them, and re-layouts  5.37 us (6%)
    pallas_call x1, Pallas kernels, on_device(): pl.pallas_call(functools.partial(kernel, (nx, ny, nz, rows, size)), out_s...  86.3 us
    unnamed x12, local copies, waits for them, and re-layouts  5.37 us

profile of v1, /device:TPU:1, one launch (start us, length us, event | category | flops | bytes accessed | tf_op | source)
XLA Modules:
  0.0 92.3 jit_solution(17553112379293170553)
XLA Ops:
  0.6 0.0 copy-start.4
  0.6 0.6 copy-done.4
  1.3 0.0 copy-start
  1.3 1.0 %copy-done = f32[16,2,16,256]{3,2,1,0:T(8,128)S(1)} copy-done((f32[16,2,16,256]{3,2,1,0:T(8,128)S(1)}, f32[16,2,16,256]{3,2,1,0:T(8,128)}, u32[]{:S(2)}) %copy-start) | copy-done | bytes 524312
  2.3 0.0 copy-start.1
  2.3 0.8 copy-done.1
  3.1 0.0 copy-start.2
  3.1 0.8 copy-done.2
  3.8 0.0 copy-start.3
  3.8 0.8 copy-done.3
  4.6 86.3 %shard_map.68 = (f32[16,2,16,256]{3,2,1,0:T(8,128)S(1)}, f32[2,16,256]{2,1,0:T(8,128)S(1)}) custom-call(f32[16,32,256]{2,1,0:T(8,128)S(1)} %bitcast.1, f32[2,16,256]{2,1,0:T(8,128)S(1)} %copy-done.1, f32[2,16,256]{2,1,0:T(8,128)S(1)} %copy-done.2, f32[16]{0:T(128)S(1)} %copy-done.4, f32[16,512]{1,0:T(8,128)S(1)} %copy-done.3), custom_call_target="tpu_custom_call" | custom-call | tf_op jit(solution)/shard_map/pallas_call | solution.py:299
  90.9 0.8 copy.9
  91.7 0.6 copy.10
Async XLA Ops:
  0.6 0.7 copy-start.4
  1.3 1.0 %copy-start = (f32[16,2,16,256]{3,2,1,0:T(8,128)S(1)}, f32[16,2,16,256]{3,2,1,0:T(8,128)}, u32[]{:S(2)}) copy-start(f32[16,2,16,256]{3,2,1,0:T(8,128)} %param.5) | copy-start | bytes 1572868
  2.3 0.8 copy-start.1
  3.1 0.8 copy-start.2
  3.8 0.8 copy-start.3

commit v2 on v1

v2 whole, which is shorter than its diff:
```python
import functools

import jax
import jax.numpy as jnp
from jax import lax
from jax.experimental import pallas as pl
from jax.experimental.pallas import tpu as pltpu
from jax.sharding import PartitionSpec as P

MESH = pl.DeviceIdType.MESH
time_step = 0.1
field_weight = 0.0625
LANES = 128
CORES = 2
F32 = jnp.float32
BF16 = jnp.bfloat16


def split(value):
    high = value.astype(BF16)
    return high, (value - high.astype(F32)).astype(BF16)


def dot(first, second):
    return jnp.dot(first, second, preferred_element_type=F32)


def dot3(first, second):
    return dot(first[0], second[0]) + (dot(first[0], second[1]) + dot(first[1], second[0]))


def wait_for(ref, sem):
    pltpu.make_async_copy(ref, ref, sem).wait()


def kernel(
    dims,
    gin_hbm, dens_hbm, bare_hbm, coup, prop_hbm,
    out, dout,
    gin, dens, bare, prop, stage, got, abuf, ah, al, hb, zbuf, shares, shared, sd, mixed, back, stage2, whole, final, summed, hl, hr,
    send, recv, load,
):
    nx, ny, nz, rows, size = dims
    nmode, norb = nx * ny, nz * CORES
    modes = nmode * norb
    half = norb // 2
    cols = size // 2
    PROP_Y, PROP_X, PROP_C = 0, 0, nx
    base = 2 * nx
    ENTRY, MIXED, WHOLE = base, base + 2, base + 4
    FIELD_Z, FIELD_C, RESULT, FIRST = base + 6, base + 7, base + 8, base + 9
    SUM_Z, SUM_Y, SUM_X, SUM_C = base + 10, base + 12, base + 14, base + 16
    mu, om = lax.axis_index("mode"), lax.axis_index("orb")
    px, py = mu // ny, mu % ny
    pz, core = om // CORES, om % CORES
    other = 1 - core
    pair = pz * CORES + other

    def push(src, dst, index, target):
        pltpu.make_async_remote_copy(
            src_ref=src, dst_ref=dst, send_sem=send.at[index], recv_sem=recv.at[index],
            device_id=target, device_id_type=MESH,
        ).start()

    pending = []

    def arrive(ref, index):
        wait_for(ref, recv.at[index])

    def each(count, body):
        def step(k, carry):
            body(k)
            return carry
        lax.fori_loop(1, count, step, 0)

    loads = [
        pltpu.make_async_copy(src, dst, load.at[i])
        for i, (src, dst) in enumerate(
            ((prop_hbm, prop), (gin_hbm, gin), (bare_hbm, bare), (dens_hbm, dens))
        )
    ]
    for copy in loads:
        copy.start()

    barrier = pltpu.get_barrier_semaphore()

    def greet_mode(k):
        pl.semaphore_signal(barrier, inc=1, device_id=((mu + k) % nmode, om), device_id_type=MESH)

    def greet_orb(k):
        pl.semaphore_signal(barrier, inc=1, device_id=(mu, (om + k) % norb), device_id_type=MESH)

    each(nmode, greet_mode)
    each(norb, greet_orb)

    loads[0].wait()
    abuf[core, mu, :, :modes] = prop[pl.ds(pl.multiple_of(core * half, half), half), :]
    lines = lax.broadcasted_iota(jnp.int32, (half, LANES), 0)
    tile = jnp.zeros((half, LANES), F32)
    for j in range(half):
        tile = jnp.where(lines == j, coup[core * half + j], tile)
    abuf[core, mu, :, modes:] = tile
    loads[2].wait()
    loads[3].wait()
    for part in range(2):
        hb[part, pz, core] = bare[part] + field_weight * dens[part]
        hb[2 + part, pz, core] = dens[part]
    loads[1].wait()
    for h in range(2):
        stage[h] = jnp.swapaxes(gin[:, :, h * cols : (h + 1) * cols], 0, 1)

    share = coup[0] * gin[0]
    for i in range(1, norb):
        share = share + coup[i] * gin[i]
    shares[...] = share[:, None, :]

    pl.semaphore_wait(barrier, nmode + norb - 2)

    def send_prop_y(k):
        push(abuf.at[core, mu], abuf.at[core, mu], PROP_Y, (px * ny + (py + k) % ny, om))

    each(ny, send_prop_y)
    pending.append((abuf.at[0, pl.ds(0, ny - 1)], PROP_Y))

    def send_entries(h, k):
        nu = (mu + k) % nmode
        push(stage.at[h, nu], got.at[h, mu], ENTRY + h, (nu, om))

    def send_fields(k):
        target = (pz + k) % nz
        push(hb.at[:, pz, core], hb.at[:, pz, core], FIELD_Z, (mu, target * CORES + core))

    each(nmode, functools.partial(send_entries, 0))
    pending.append((got.at[0, pl.ds(0, nmode - 1)], ENTRY))

    def span_of(d):
        return pl.ds(pl.multiple_of((px - d + nx) % nx * ny, ny), ny)

    order = [0, 1] + list(range(nx - 1, 1, -1))
    group = span_of(0)

    def cross(d):
        push(abuf.at[core, span_of(d)], abuf.at[core, span_of(d)], PROP_C + d, (mu, pair))
        pending.append((abuf.at[0, pl.ds(0, ny)], PROP_C + d))

    arrive(abuf.at[0, pl.ds(0, ny - 1)], PROP_Y)
    for d in order[1:]:
        push(abuf.at[core, group], abuf.at[core, group], PROP_X + d, ((px + d) % nx * ny + py, om))
        pending.append((abuf.at[0, pl.ds(0, ny)], PROP_X + d))
    cross(0)
    each(nmode, functools.partial(send_entries, 1))
    pending.append((got.at[1, pl.ds(0, nmode - 1)], ENTRY + 1))

    def send_share(k):
        nu = (mu + k) % nmode
        push(shares.at[nu], shared.at[mu], FIRST, (nu, om))

    each(nmode, send_share)
    pending.append((shared.at[pl.ds(0, nmode - 1)], FIRST))
    each(nz, send_fields)
    pending.append((hb.at[:, pl.ds(0, nz - 1), 0], FIELD_Z))
    shared[mu] = shares[mu]
    for h in range(2):
        got[h, mu] = stage[h, mu]
    for d in order[1:]:
        arrive(abuf.at[0, pl.ds(0, ny)], PROP_X + d)
        cross(d)

    def matrix(part):
        return hb[part].reshape(size, size)

    def store_h(step, real, imag):
        rh, rl = split(time_step * real)
        ih, il = split(time_step * imag)
        for level, (r, i) in enumerate(((rh, ih), (rl, il))):
            hl[step, level, :size, :size] = r
            hl[step, level, size:, size:] = r
            hl[step, level, :size, size:] = -i
            hl[step, level, size:, :size] = i
            hr[step, level, :size, :size] = r
            hr[step, level, size:, size:] = r
            hr[step, level, :size, size:] = i
            hr[step, level, size:, :size] = -i

    def turn(step, real, imag):
        rh, rl = split(real)
        ih, il = split(imag)
        left = dot3(
            (hl[step, 0], hl[step, 1]),
            (jnp.concatenate([rh, ih], 0), jnp.concatenate([rl, il], 0)),
        )
        right = dot3(
            (jnp.concatenate([rh, ih], 1), jnp.concatenate([rl, il], 1)),
            (hr[step, 0], hr[step, 1]),
        )
        return (
            real + (left[size:] - right[:, size:]),
            imag - (left[:size] - right[:, :size]),
        )

    def unpack(d):
        arrive(abuf.at[0, pl.ds(0, ny)], PROP_C + d)

        def step(j, carry):
            k = (px - d + nx) % nx * ny + j
            block = jnp.concatenate([abuf[0, k, :, :modes], abuf[1, k, :, :modes]], 0)
            high, low = split(block)
            where = pl.ds(pl.multiple_of(k * norb, norb), norb)
            ah[where, :] = high
            al[where, :] = low
            return carry

        lax.fori_loop(0, ny, step, 0)

    def mix(h):
        high, low = split(got[h].reshape(modes, cols))
        span = ny * norb
        for d in order:
            if h == 0:
                unpack(d)
            first = (px - d + nx) % nx
            where = pl.ds(pl.multiple_of(first * span, span), span)
            mixed[h, where, :] = dot3((ah[where, :], al[where, :]), (high, low))

            def send_mixed(k, first=first):
                nu = first * ny + (py + k) % ny
                rows_of = pl.ds(pl.multiple_of(nu * norb, norb), norb)
                push(mixed.at[h, rows_of], back.at[h, mu], MIXED + h, (nu, om))

            if d:
                send_mixed(0)
            each(ny, send_mixed)
        back[h, mu] = mixed[h, pl.ds(pl.multiple_of(mu * norb, norb), norb), :]
        pending.append((back.at[h, pl.ds(0, nmode - 1)], MIXED + h))

    def sums_z(which, row):
        zbuf[which, pz] = row

        def send_sums(k):
            target = (mu, (pz + k) % nz * CORES + core)
            push(zbuf.at[which, pz], zbuf.at[which, pz], SUM_Z + which, target)

        each(nz, send_sums)
        pending.append((zbuf.at[which, pl.ds(0, nz - 1)], SUM_Z + which))

    def sums_y(which):
        arrive(zbuf.at[which, pl.ds(0, nz - 1)], SUM_Z + which)
        sd[which, core, mu] = zbuf[which][:, 0, :]

        def send_sums(k):
            target = (px * ny + (py + k) % ny, om)
            push(sd.at[which, core, mu], sd.at[which, core, mu], SUM_Y + which, target)

        each(ny, send_sums)
        pending.append((sd.at[which, 0, pl.ds(0, ny - 1)], SUM_Y + which))

    def sums_x(which):
        arrive(sd.at[which, 0, pl.ds(0, ny - 1)], SUM_Y + which)

        def send_sums(k):
            target = ((px + k) % nx * ny + py, om)
            push(sd.at[which, core, group], sd.at[which, core, group], SUM_X + which, target)

        each(nx, send_sums)
        pending.append((sd.at[which, 0, pl.ds(0, (nx - 1) * ny)], SUM_X + which))

    def sums_core(which):
        arrive(sd.at[which, 0, pl.ds(0, (nx - 1) * ny)], SUM_X + which)
        push(sd.at[which, core], sd.at[which, core], SUM_C + which, (mu, pair))
        pending.append((sd.at[which, 0], SUM_C + which))

    def sums_all(which):
        arrive(sd.at[which, 0], SUM_C + which)
        for side in range(2):
            for part in range(2):
                block = jnp.swapaxes(sd[which, side, part * rows : (part + 1) * rows], 0, 1)
                summed[part, :, side] = block
        return tuple(summed[part].reshape(size, size) for part in range(2))

    arrive(shared.at[pl.ds(0, nmode - 1)], FIRST)
    sums_z(0, jnp.sum(shared[...], axis=0))
    arrive(got.at[0, pl.ds(0, nmode - 1)], ENTRY)
    mix(0)
    sums_y(0)
    arrive(hb.at[:, pl.ds(0, nz - 1), 0], FIELD_Z)
    push(hb.at[:, :, core], hb.at[:, :, core], FIELD_C, (mu, pair))
    pending.append((hb.at[:, :, 0], FIELD_C))
    arrive(got.at[1, pl.ds(0, nmode - 1)], ENTRY + 1)
    mix(1)
    sums_x(0)
    weights = jnp.concatenate(
        [abuf[0, :, :, modes:][:, None], abuf[1, :, :, modes:][:, None]], 1
    ).reshape(modes, LANES)
    wide = weights[:, :cols]
    own = prop[pl.ds(om, 1), :]
    sums_z(1, jnp.concatenate(
        [jnp.sum(wide * mixed[h], axis=0, keepdims=True) for h in range(2)], 1
    ))

    def spread(h):
        arrive(back.at[h, pl.ds(0, nmode - 1)], MIXED + h)
        stage2[h] = jnp.swapaxes(back[h], 0, 1).reshape(norb, 2, rows, cols)

        def send_matrix(k):
            target = (om + k) % norb
            push(stage2.at[h, target], whole.at[h, :, om], WHOLE + h, (mu, target))

        each(norb, send_matrix)
        whole[h, :, om] = stage2[h, om]
        pending.append((whole.at[h, :, pl.ds(0, norb - 1)], WHOLE + h))

    column = jnp.sum(weights[:, :1] * (ah[...].astype(F32) + al[...].astype(F32)), axis=0, keepdims=True)
    both = jnp.concatenate([own, column, jnp.zeros((6, modes), F32)], 0)
    products = jnp.dot(both, weights, precision=lax.Precision.HIGHEST, preferred_element_type=F32)
    e_own = products[0:1, 0:1]
    f_all = products[1:2, 0:1]
    c_all = jnp.sum(weights * weights, axis=0, keepdims=True)[:, :1]
    c_own = coup[om]
    arrive(hb.at[:, :, 0], FIELD_C)
    store_h(0, matrix(0), matrix(1))

    spread(0)
    sums_core(0)
    sums_y(1)

    source = sums_all(0)
    densities = [(matrix(2), matrix(3))]
    fields = tuple(matrix(part) for part in range(2))
    for step in range(2):
        source = turn(step, *source)
        source = tuple(source[p] + (c_all * time_step) * densities[step][p] for p in range(2))
        densities.append(tuple(densities[step][p] + time_step * source[p] for p in range(2)))
        fields = tuple(fields[p] + (field_weight * time_step) * source[p] for p in range(2))
        store_h(step + 1, *fields)

    spread(1)
    sums_x(1)
    for h in range(2):
        arrive(whole.at[h, :, pl.ds(0, norb - 1)], WHOLE + h)
    state = tuple(
        jnp.concatenate([whole[h, part].reshape(size, cols) for h in range(2)], 1)
        for part in range(2)
    )
    for step in range(3):
        weight = e_own if step < 2 else c_own
        state = turn(step, *state)
        state = tuple(state[p] + (weight * time_step) * densities[step][p] for p in range(2))
    for part in range(2):
        final[part] = state[part].reshape(norb, rows, size)

    def send_result(k):
        target = (om + k) % norb
        push(final.at[:, target], out.at[om], RESULT, (mu, target))

    each(norb, send_result)
    pending.append((out.at[pl.ds(0, norb - 1)], RESULT))
    out[om] = final[:, om]

    sums_core(1)
    chain = sums_all(1)
    for step in range(3):
        weight = f_all if step < 2 else c_all
        chain = turn(step, *chain)
        chain = tuple(chain[p] + (weight * time_step) * densities[step][p] for p in range(2))
    for part in range(2):
        summed[part] = (densities[2][part] + time_step * chain[part]).reshape(nz, CORES, rows, size)
    for part in range(2):
        dout[part] = summed[part, pz, core]

    arrive(out.at[pl.ds(0, norb - 1)], RESULT)
    for ref, index in pending:
        wait_for(ref, send.at[index])


def build(mesh, nx, ny):
    def on_device(correlators, density, bare_hamiltonian, coupling, propagator):
        local, _, rows, size = correlators.shape
        nmode, norb = mesh.shape["mode"], mesh.shape["orb"]
        nz = norb // CORES
        modes = nmode * norb
        vmem = pl.BlockSpec(memory_space=pltpu.VMEM)
        whole = pl.BlockSpec(memory_space=pltpu.HBM)
        return pl.pallas_call(
            functools.partial(kernel, (nx, ny, nz, rows, size)),
            out_shape=(
                jax.ShapeDtypeStruct(correlators.shape, F32),
                jax.ShapeDtypeStruct(density.shape, F32),
            ),
            in_specs=[whole, whole, whole, pl.BlockSpec(memory_space=pltpu.SMEM), whole],
            out_specs=(vmem, vmem),
            scratch_shapes=[
                pltpu.VMEM((local, 2 * rows, size), F32),
                pltpu.VMEM(density.shape, F32),
                pltpu.VMEM(density.shape, F32),
                pltpu.VMEM(propagator.shape, F32),
                pltpu.VMEM((2, nmode, norb, size // 2), F32),
                pltpu.VMEM((2, nmode, norb, size // 2), F32),
                pltpu.VMEM((2, nmode, norb // 2, modes + LANES), F32),
                pltpu.VMEM((modes, modes), BF16),
                pltpu.VMEM((modes, modes), BF16),
                pltpu.VMEM((4, nz, CORES, rows, size), F32),
                pltpu.VMEM((2, nz, 1, size), F32),
                pltpu.VMEM((nmode, 1, size), F32),
                pltpu.VMEM((nmode, 1, size), F32),
                pltpu.VMEM((2, 2, nmode, nz, size), F32),
                pltpu.VMEM((2, modes, size // 2), F32),
                pltpu.VMEM((2, nmode, norb, size // 2), F32),
                pltpu.VMEM((2, norb, 2, rows, size // 2), F32),
                pltpu.VMEM((2, 2, norb, rows, size // 2), F32),
                pltpu.VMEM((2, norb, rows, size), F32),
                pltpu.VMEM((2, nz, CORES, rows, size), F32),
                pltpu.VMEM((3, 2, 2 * size, 2 * size), BF16),
                pltpu.VMEM((3, 2, 2 * size, 2 * size), BF16),
                pltpu.SemaphoreType.DMA((2 * nx + 18,)),
                pltpu.SemaphoreType.DMA((2 * nx + 18,)),
                pltpu.SemaphoreType.DMA((4,)),
            ],
            compiler_params=pltpu.CompilerParams(
                collective_id=0, has_side_effects=True, vmem_limit_bytes=60 * 1024 * 1024
            ),
        )(
            correlators.reshape(local, 2 * rows, size),
            density, bare_hamiltonian, coupling, propagator,
        )

    in_specs = (
        P("mode", None, "orb", None),
        P(None, "orb", None),
        P(None, "orb", None),
        P("mode"),
        P("mode", None),
    )
    out_specs = (P("mode", None, "orb", None), P(None, "orb", None))
    return jax.shard_map(
        on_device, mesh=mesh, in_specs=in_specs, out_specs=out_specs, check_vma=False
    )


def solution(mesh):
    return build(mesh, 4, mesh.shape["mode"] // 4)
```

time: 92.7 us -> 86.4 us (0.932)
  Pallas kernels: 86.3 us -> 83.1 us
  local copies, waits for them, and re-layouts: 5.37 us -> 2.51 us
    pallas_call x1, Pallas kernels: 86.3 us -> 83.1 us  [on_device(): pl.pallas_call(functools.partial(kernel, (nx, ny, nz, rows, size)), out_s...]
    unnamed x12 -> x4, local copies, waits for them, and re-layouts: 5.37 us -> 2.51 us
where the time goes in v2:
time: 86.4 us; the launch traced here: 86.3 us
  Pallas kernels  83.1 us (96%)
  local copies, waits for them, and re-layouts  2.51 us (3%)
    pallas_call x1, Pallas kernels, on_device(): pl.pallas_call(functools.partial(kernel, (nx, ny, nz, rows, size)), out_s...  83.1 us
    unnamed x4, local copies, waits for them, and re-layouts  2.51 us

profile of v2, /device:TPU:1, one launch (start us, length us, event | category | flops | bytes accessed | tf_op | source)
XLA Modules:
  0.0 86.3 jit_solution(6255365532151625180)
XLA Ops:
  0.6 83.1 %shard_map.68 = (f32[16,2,16,256]{3,2,1,0:T(8,128)}, f32[2,16,256]{2,1,0:T(8,128)}) custom-call(f32[16,32,256]{2,1,0:T(8,128)} %bitcast.1, f32[2,16,256]{2,1,0:T(8,128)} %dens_hbm.1, f32[2,16,256]{2,1,0:T(8,128)} %bare_hbm.1, f32[16]{0:T(128)} %coup.1, f32[16,512]{1,0:T(8,128)} %prop_hbm.1), custom_call_target="tpu_custom_call" | custom-call | tf_op jit(solution)/shard_map/pallas_call | solution.py:383
  83.8 0.0 copy-start
  83.8 1.9 %copy.9 = f32[16,2,16,256]{3,2,1,0:T(8,128)} copy(f32[16,2,16,256]{3,2,1,0:T(8,128)} %get-tuple-element.4) | data formatting | bytes 1048576
  85.7 0.0 copy-done
  85.7 0.6 copy.10
Async XLA Ops:
  83.8 1.9 %copy-start = (f32[2,16,256]{2,1,0:T(8,128)S(1)}, f32[2,16,256]{2,1,0:T(8,128)}, u32[]{:S(2)}) copy-start(f32[2,16,256]{2,1,0:T(8,128)} %get-tuple-element.5) | copy-start | bytes 98308

commit v3 on v2

--- a/solution.py
+++ b/solution.py
@@ -50,6 +50,7 @@
     ENTRY, MIXED, WHOLE = base, base + 2, base + 4
     FIELD_Z, FIELD_C, RESULT, FIRST = base + 6, base + 7, base + 8, base + 9
     SUM_Z, SUM_Y, SUM_X, SUM_C = base + 10, base + 12, base + 14, base + 16
+    NEAR_MIXED, NEAR_WHOLE = base + 18, base + 19
     mu, om = lax.axis_index("mode"), lax.axis_index("orb")
     px, py = mu // ny, mu % ny
     pz, core = om // CORES, om % CORES
@@ -94,48 +95,35 @@
     each(norb, greet_orb)
 
     loads[0].wait()
-    abuf[core, mu, :, :modes] = prop[pl.ds(pl.multiple_of(core * half, half), half), :]
-    lines = lax.broadcasted_iota(jnp.int32, (half, LANES), 0)
-    tile = jnp.zeros((half, LANES), F32)
-    for j in range(half):
-        tile = jnp.where(lines == j, coup[core * half + j], tile)
-    abuf[core, mu, :, modes:] = tile
-    loads[2].wait()
-    loads[3].wait()
-    for part in range(2):
-        hb[part, pz, core] = bare[part] + field_weight * dens[part]
-        hb[2 + part, pz, core] = dens[part]
+    abuf[core, mu] = prop[pl.ds(pl.multiple_of(core * half, half), half), :]
+    pl.semaphore_wait(barrier, nmode + norb - 2)
+
+    def send_prop_y(k):
+        push(abuf.at[core, mu], abuf.at[core, mu], PROP_Y, (px * ny + (py + k) % ny, om))
+
+    each(ny, send_prop_y)
+    pending.append((abuf.at[0, pl.ds(0, ny - 1)], PROP_Y))
+
+    def send_entries(h, k):
+        nu = (mu + k) % nmode
+        push(stage.at[h, nu], got.at[h, mu], ENTRY + h, (nu, om))
+
+    def send_fields(k):
+        target = (pz + k) % nz
+        push(hb.at[:, pz, core], hb.at[:, pz, core], FIELD_Z, (mu, target * CORES + core))
+
     loads[1].wait()
     for h in range(2):
         stage[h] = jnp.swapaxes(gin[:, :, h * cols : (h + 1) * cols], 0, 1)
-
-    share = coup[0] * gin[0]
-    for i in range(1, norb):
-        share = share + coup[i] * gin[i]
-    shares[...] = share[:, None, :]
-
-    pl.semaphore_wait(barrier, nmode + norb - 2)
-
-    def send_prop_y(k):
-        push(abuf.at[core, mu], abuf.at[core, mu], PROP_Y, (px * ny + (py + k) % ny, om))
-
-    each(ny, send_prop_y)
-    pending.append((abuf.at[0, pl.ds(0, ny - 1)], PROP_Y))
-
-    def send_entries(h, k):
-        nu = (mu + k) % nmode
-        push(stage.at[h, nu], got.at[h, mu], ENTRY + h, (nu, om))
-
-    def send_fields(k):
-        target = (pz + k) % nz
-        push(hb.at[:, pz, core], hb.at[:, pz, core], FIELD_Z, (mu, target * CORES + core))
-
-    each(nmode, functools.partial(send_entries, 0))
+        if h == 0:
+            each(nmode, functools.partial(send_entries, 0))
     pending.append((got.at[0, pl.ds(0, nmode - 1)], ENTRY))
 
     def span_of(d):
         return pl.ds(pl.multiple_of((px - d + nx) % nx * ny, ny), ny)
 
+    near = om // half
+    sides = (1 - near, near)
     order = [0, 1] + list(range(nx - 1, 1, -1))
     group = span_of(0)
 
@@ -151,12 +139,26 @@
     each(nmode, functools.partial(send_entries, 1))
     pending.append((got.at[1, pl.ds(0, nmode - 1)], ENTRY + 1))
 
+    share = coup[0] * gin[0]
+    for i in range(1, norb):
+        share = share + coup[i] * gin[i]
+    lanes = lax.broadcasted_iota(jnp.int32, (nmode, LANES), 1)
+    line = jnp.zeros((nmode, LANES), F32)
+    for i in range(norb):
+        line = jnp.where(lanes == i, coup[i], line)
+    shares[...] = jnp.concatenate([share, line], 1)[:, None, :]
+
     def send_share(k):
         nu = (mu + k) % nmode
         push(shares.at[nu], shared.at[mu], FIRST, (nu, om))
 
     each(nmode, send_share)
     pending.append((shared.at[pl.ds(0, nmode - 1)], FIRST))
+    loads[2].wait()
+    loads[3].wait()
+    for part in range(2):
+        hb[part, pz, core] = bare[part] + field_weight * dens[part]
+        hb[2 + part, pz, core] = dens[part]
     each(nz, send_fields)
     pending.append((hb.at[:, pl.ds(0, nz - 1), 0], FIELD_Z))
     shared[mu] = shares[mu]
@@ -203,7 +205,7 @@
 
         def step(j, carry):
             k = (px - d + nx) % nx * ny + j
-            block = jnp.concatenate([abuf[0, k, :, :modes], abuf[1, k, :, :modes]], 0)
+            block = jnp.concatenate([abuf[0, k], abuf[1, k]], 0)
             high, low = split(block)
             where = pl.ds(pl.multiple_of(k * norb, norb), norb)
             ah[where, :] = high
@@ -222,16 +224,31 @@
             where = pl.ds(pl.multiple_of(first * span, span), span)
             mixed[h, where, :] = dot3((ah[where, :], al[where, :]), (high, low))
 
+            if h:
+                continue
+
             def send_mixed(k, first=first):
                 nu = first * ny + (py + k) % ny
                 rows_of = pl.ds(pl.multiple_of(nu * norb, norb), norb)
-                push(mixed.at[h, rows_of], back.at[h, mu], MIXED + h, (nu, om))
+                push(mixed.at[h, rows_of], back.at[h, mu], MIXED, (nu, om))
 
             if d:
                 send_mixed(0)
             each(ny, send_mixed)
+        for side in range(2 * h):
+            start = sides[side] * half
+
+            def send_part(k):
+                nu = (mu + k) % nmode
+                rows_of = pl.ds(pl.multiple_of(nu * norb + start, half), half)
+                there = back.at[h, mu, pl.ds(pl.multiple_of(start, half), half)]
+                push(mixed.at[h, rows_of], there, (MIXED + 1, NEAR_MIXED)[side], (nu, om))
+
+            each(nmode, send_part)
+            pending.append((back.at[h, pl.ds(0, nmode - 1), pl.ds(0, half)], (MIXED + 1, NEAR_MIXED)[side]))
         back[h, mu] = mixed[h, pl.ds(pl.multiple_of(mu * norb, norb), norb), :]
-        pending.append((back.at[h, pl.ds(0, nmode - 1)], MIXED + h))
+        if h == 0:
+            pending.append((back.at[h, pl.ds(0, nmode - 1)], MIXED))
 
     def sums_z(which, row):
         zbuf[which, pz] = row
@@ -278,7 +295,7 @@
         return tuple(summed[part].reshape(size, size) for part in range(2))
 
     arrive(shared.at[pl.ds(0, nmode - 1)], FIRST)
-    sums_z(0, jnp.sum(shared[...], axis=0))
+    sums_z(0, jnp.sum(shared[:, :, :size], axis=0))
     arrive(got.at[0, pl.ds(0, nmode - 1)], ENTRY)
     mix(0)
     sums_y(0)
@@ -288,9 +305,13 @@
     arrive(got.at[1, pl.ds(0, nmode - 1)], ENTRY + 1)
     mix(1)
     sums_x(0)
-    weights = jnp.concatenate(
-        [abuf[0, :, :, modes:][:, None], abuf[1, :, :, modes:][:, None]], 1
-    ).reshape(modes, LANES)
+    tall = jnp.broadcast_to(shared[:, :, size:], (nmode, norb, LANES)).reshape(modes, LANES)
+    at_lane = lax.broadcasted_iota(jnp.int32, (modes, LANES), 1)
+    at_row = lax.broadcasted_iota(jnp.int32, (modes, LANES), 0)
+    weights = jnp.dot(
+        jnp.where(at_lane == at_row % norb, tall, 0.0), jnp.ones((LANES, LANES), F32),
+        precision=lax.Precision.HIGHEST, preferred_element_type=F32,
+    )
     wide = weights[:, :cols]
     own = prop[pl.ds(om, 1), :]
     sums_z(1, jnp.concatenate(
@@ -308,6 +329,25 @@
         each(norb, send_matrix)
         whole[h, :, om] = stage2[h, om]
         pending.append((whole.at[h, :, pl.ds(0, norb - 1)], WHOLE + h))
+
+    def spread_side(side):
+        arrive(back.at[1, pl.ds(0, nmode - 1), pl.ds(0, half)], (MIXED + 1, NEAR_MIXED)[side])
+        start = pl.multiple_of(sides[side] * half, half)
+        block = jnp.swapaxes(back[1, :, pl.ds(start, half), :], 0, 1)
+        stage2[1, pl.ds(start, half)] = block.reshape(half, 2, rows, cols)
+        index = (WHOLE + 1, NEAR_WHOLE)[side]
+
+        def send_matrix(k):
+            target = start + (om + k) % half
+            push(stage2.at[1, target], whole.at[1, :, om], index, (mu, target))
+
+        if side == 0:
+            send_matrix(0)
+        each(half, send_matrix)
+        count = half - side
+        pending.append((whole.at[1, :, pl.ds(0, count)], index))
+        if side:
+            whole[1, :, om] = stage2[1, om]
 
     column = jnp.sum(weights[:, :1] * (ah[...].astype(F32) + al[...].astype(F32)), axis=0, keepdims=True)
     both = jnp.concatenate([own, column, jnp.zeros((6, modes), F32)], 0)
@@ -323,6 +363,10 @@
     sums_core(0)
     sums_y(1)
 
+    spread_side(0)
+    spread_side(1)
+    sums_x(1)
+
     source = sums_all(0)
     densities = [(matrix(2), matrix(3))]
     fields = tuple(matrix(part) for part in range(2))
@@ -333,10 +377,9 @@
         fields = tuple(fields[p] + (field_weight * time_step) * source[p] for p in range(2))
         store_h(step + 1, *fields)
 
-    spread(1)
-    sums_x(1)
-    for h in range(2):
-        arrive(whole.at[h, :, pl.ds(0, norb - 1)], WHOLE + h)
+    arrive(whole.at[0, :, pl.ds(0, norb - 1)], WHOLE)
+    arrive(whole.at[1, :, pl.ds(0, half)], WHOLE + 1)
+    arrive(whole.at[1, :, pl.ds(0, half - 1)], NEAR_WHOLE)
     state = tuple(
         jnp.concatenate([whole[h, part].reshape(size, cols) for h in range(2)], 1)
         for part in range(2)
@@ -395,13 +438,13 @@
                 pltpu.VMEM(propagator.shape, F32),
                 pltpu.VMEM((2, nmode, norb, size // 2), F32),
                 pltpu.VMEM((2, nmode, norb, size // 2), F32),
-                pltpu.VMEM((2, nmode, norb // 2, modes + LANES), F32),
+                pltpu.VMEM((2, nmode, norb // 2, modes), F32),
                 pltpu.VMEM((modes, modes), BF16),
                 pltpu.VMEM((modes, modes), BF16),
                 pltpu.VMEM((4, nz, CORES, rows, size), F32),
                 pltpu.VMEM((2, nz, 1, size), F32),
-                pltpu.VMEM((nmode, 1, size), F32),
-                pltpu.VMEM((nmode, 1, size), F32),
+                pltpu.VMEM((nmode, 1, size + LANES), F32),
+                pltpu.VMEM((nmode, 1, size + LANES), F32),
                 pltpu.VMEM((2, 2, nmode, nz, size), F32),
                 pltpu.VMEM((2, modes, size // 2), F32),
                 pltpu.VMEM((2, nmode, norb, size // 2), F32),
@@ -411,8 +454,8 @@
                 pltpu.VMEM((2, nz, CORES, rows, size), F32),
                 pltpu.VMEM((3, 2, 2 * size, 2 * size), BF16),
                 pltpu.VMEM((3, 2, 2 * size, 2 * size), BF16),
-                pltpu.SemaphoreType.DMA((2 * nx + 18,)),
-                pltpu.SemaphoreType.DMA((2 * nx + 18,)),
+                pltpu.SemaphoreType.DMA((2 * nx + 20,)),
+                pltpu.SemaphoreType.DMA((2 * nx + 20,)),
                 pltpu.SemaphoreType.DMA((4,)),
             ],
             compiler_params=pltpu.CompilerParams(

time: 86.4 us -> 82.2 us (0.951)
  Pallas kernels: 83.1 us -> 78.9 us
    pallas_call x1, Pallas kernels: 83.1 us -> 78.9 us  [on_device(): pl.pallas_call(functools.partial(kernel, (nx, ny, nz, rows, size)), out_s...]
where the time goes in v3:
time: 82.2 us; the launch traced here: 82 us
  Pallas kernels  78.9 us (96%)
  local copies, waits for them, and re-layouts  2.51 us (3%)
    pallas_call x1, Pallas kernels, on_device(): pl.pallas_call(functools.partial(kernel, (nx, ny, nz, rows, size)), out_s...  78.9 us
    unnamed x4, local copies, waits for them, and re-layouts  2.51 us

profile of v3, /device:TPU:1, one launch (start us, length us, event | category | flops | bytes accessed | tf_op | source)
XLA Modules:
  0.0 82.0 jit_solution(15924691281633481784)
XLA Ops:
  0.6 78.9 %shard_map.68 = (f32[16,2,16,256]{3,2,1,0:T(8,128)}, f32[2,16,256]{2,1,0:T(8,128)}) custom-call(f32[16,32,256]{2,1,0:T(8,128)} %bitcast.1, f32[2,16,256]{2,1,0:T(8,128)} %dens_hbm.1, f32[2,16,256]{2,1,0:T(8,128)} %bare_hbm.1, f32[16]{0:T(128)} %coup.1, f32[16,512]{1,0:T(8,128)} %prop_hbm.1), custom_call_target="tpu_custom_call" | custom-call | tf_op jit(solution)/shard_map/pallas_call | solution.py:426
  79.5 0.0 copy-start
  79.5 1.9 %copy.9 = f32[16,2,16,256]{3,2,1,0:T(8,128)} copy(f32[16,2,16,256]{3,2,1,0:T(8,128)} %get-tuple-element.4) | data formatting | bytes 1048576
  81.4 0.0 copy-done
  81.4 0.6 copy.10
Async XLA Ops:
  79.5 1.9 %copy-start = (f32[2,16,256]{2,1,0:T(8,128)S(1)}, f32[2,16,256]{2,1,0:T(8,128)}, u32[]{:S(2)}) copy-start(f32[2,16,256]{2,1,0:T(8,128)} %get-tuple-element.5) | copy-start | bytes 98308

commit v4 on v3

--- a/solution.py
+++ b/solution.py
@@ -113,32 +113,6 @@
         push(hb.at[:, pz, core], hb.at[:, pz, core], FIELD_Z, (mu, target * CORES + core))
 
     loads[1].wait()
-    for h in range(2):
-        stage[h] = jnp.swapaxes(gin[:, :, h * cols : (h + 1) * cols], 0, 1)
-        if h == 0:
-            each(nmode, functools.partial(send_entries, 0))
-    pending.append((got.at[0, pl.ds(0, nmode - 1)], ENTRY))
-
-    def span_of(d):
-        return pl.ds(pl.multiple_of((px - d + nx) % nx * ny, ny), ny)
-
-    near = om // half
-    sides = (1 - near, near)
-    order = [0, 1] + list(range(nx - 1, 1, -1))
-    group = span_of(0)
-
-    def cross(d):
-        push(abuf.at[core, span_of(d)], abuf.at[core, span_of(d)], PROP_C + d, (mu, pair))
-        pending.append((abuf.at[0, pl.ds(0, ny)], PROP_C + d))
-
-    arrive(abuf.at[0, pl.ds(0, ny - 1)], PROP_Y)
-    for d in order[1:]:
-        push(abuf.at[core, group], abuf.at[core, group], PROP_X + d, ((px + d) % nx * ny + py, om))
-        pending.append((abuf.at[0, pl.ds(0, ny)], PROP_X + d))
-    cross(0)
-    each(nmode, functools.partial(send_entries, 1))
-    pending.append((got.at[1, pl.ds(0, nmode - 1)], ENTRY + 1))
-
     share = coup[0] * gin[0]
     for i in range(1, norb):
         share = share + coup[i] * gin[i]
@@ -154,6 +128,33 @@
 
     each(nmode, send_share)
     pending.append((shared.at[pl.ds(0, nmode - 1)], FIRST))
+    shared[mu] = shares[mu]
+    for h in range(2):
+        stage[h] = jnp.swapaxes(gin[:, :, h * cols : (h + 1) * cols], 0, 1)
+        if h == 0:
+            each(nmode, functools.partial(send_entries, 0))
+    pending.append((got.at[0, pl.ds(0, nmode - 1)], ENTRY))
+
+    def span_of(d):
+        return pl.ds(pl.multiple_of((px - d + nx) % nx * ny, ny), ny)
+
+    near = om // half
+    sides = (1 - near, near)
+    order = [0, 1] + list(range(nx - 1, 1, -1))
+    group = span_of(0)
+
+    def cross(d):
+        push(abuf.at[core, span_of(d)], abuf.at[core, span_of(d)], PROP_C + d, (mu, pair))
+        pending.append((abuf.at[0, pl.ds(0, ny)], PROP_C + d))
+
+    arrive(abuf.at[0, pl.ds(0, ny - 1)], PROP_Y)
+    for d in order[1:]:
+        push(abuf.at[core, group], abuf.at[core, group], PROP_X + d, ((px + d) % nx * ny + py, om))
+        pending.append((abuf.at[0, pl.ds(0, ny)], PROP_X + d))
+    cross(0)
+    each(nmode, functools.partial(send_entries, 1))
+    pending.append((got.at[1, pl.ds(0, nmode - 1)], ENTRY + 1))
+
     loads[2].wait()
     loads[3].wait()
     for part in range(2):
@@ -161,12 +162,59 @@
         hb[2 + part, pz, core] = dens[part]
     each(nz, send_fields)
     pending.append((hb.at[:, pl.ds(0, nz - 1), 0], FIELD_Z))
-    shared[mu] = shares[mu]
     for h in range(2):
         got[h, mu] = stage[h, mu]
+
+    def sums_z(which, row):
+        zbuf[which, pz] = row
+
+        def send_sums(k):
+            target = (mu, (pz + k) % nz * CORES + core)
+            push(zbuf.at[which, pz], zbuf.at[which, pz], SUM_Z + which, target)
+
+        each(nz, send_sums)
+        pending.append((zbuf.at[which, pl.ds(0, nz - 1)], SUM_Z + which))
+
+    def sums_y(which):
+        arrive(zbuf.at[which, pl.ds(0, nz - 1)], SUM_Z + which)
+        sd[which, core, mu] = zbuf[which][:, 0, :]
+
+        def send_sums(k):
+            target = (px * ny + (py + k) % ny, om)
+            push(sd.at[which, core, mu], sd.at[which, core, mu], SUM_Y + which, target)
+
+        each(ny, send_sums)
+        pending.append((sd.at[which, 0, pl.ds(0, ny - 1)], SUM_Y + which))
+
+    def sums_x(which):
+        arrive(sd.at[which, 0, pl.ds(0, ny - 1)], SUM_Y + which)
+
+        def send_sums(k):
+            target = ((px + k) % nx * ny + py, om)
+            push(sd.at[which, core, group], sd.at[which, core, group], SUM_X + which, target)
+
+        each(nx, send_sums)
+        pending.append((sd.at[which, 0, pl.ds(0, (nx - 1) * ny)], SUM_X + which))
+
+    def sums_core(which):
+        arrive(sd.at[which, 0, pl.ds(0, (nx - 1) * ny)], SUM_X + which)
+        push(sd.at[which, core], sd.at[which, core], SUM_C + which, (mu, pair))
+        pending.append((sd.at[which, 0], SUM_C + which))
+
+    def sums_all(which):
+        arrive(sd.at[which, 0], SUM_C + which)
+        for side in range(2):
+            for part in range(2):
+                block = jnp.swapaxes(sd[which, side, part * rows : (part + 1) * rows], 0, 1)
+                summed[part, :, side] = block
+        return tuple(summed[part].reshape(size, size) for part in range(2))
+
+    arrive(shared.at[pl.ds(0, nmode - 1)], FIRST)
+    sums_z(0, jnp.sum(shared[:, :, :size], axis=0))
     for d in order[1:]:
         arrive(abuf.at[0, pl.ds(0, ny)], PROP_X + d)
         cross(d)
+    sums_y(0)
 
     def matrix(part):
         return hb[part].reshape(size, size)
@@ -250,55 +298,8 @@
         if h == 0:
             pending.append((back.at[h, pl.ds(0, nmode - 1)], MIXED))
 
-    def sums_z(which, row):
-        zbuf[which, pz] = row
-
-        def send_sums(k):
-            target = (mu, (pz + k) % nz * CORES + core)
-            push(zbuf.at[which, pz], zbuf.at[which, pz], SUM_Z + which, target)
-
-        each(nz, send_sums)
-        pending.append((zbuf.at[which, pl.ds(0, nz - 1)], SUM_Z + which))
-
-    def sums_y(which):
-        arrive(zbuf.at[which, pl.ds(0, nz - 1)], SUM_Z + which)
-        sd[which, core, mu] = zbuf[which][:, 0, :]
-
-        def send_sums(k):
-            target = (px * ny + (py + k) % ny, om)
-            push(sd.at[which, core, mu], sd.at[which, core, mu], SUM_Y + which, target)
-
-        each(ny, send_sums)
-        pending.append((sd.at[which, 0, pl.ds(0, ny - 1)], SUM_Y + which))
-
-    def sums_x(which):
-        arrive(sd.at[which, 0, pl.ds(0, ny - 1)], SUM_Y + which)
-
-        def send_sums(k):
-            target = ((px + k) % nx * ny + py, om)
-            push(sd.at[which, core, group], sd.at[which, core, group], SUM_X + which, target)
-
-        each(nx, send_sums)
-        pending.append((sd.at[which, 0, pl.ds(0, (nx - 1) * ny)], SUM_X + which))
-
-    def sums_core(which):
-        arrive(sd.at[which, 0, pl.ds(0, (nx - 1) * ny)], SUM_X + which)
-        push(sd.at[which, core], sd.at[which, core], SUM_C + which, (mu, pair))
-        pending.append((sd.at[which, 0], SUM_C + which))
-
-    def sums_all(which):
-        arrive(sd.at[which, 0], SUM_C + which)
-        for side in range(2):
-            for part in range(2):
-                block = jnp.swapaxes(sd[which, side, part * rows : (part + 1) * rows], 0, 1)
-                summed[part, :, side] = block
-        return tuple(summed[part].reshape(size, size) for part in range(2))
-
-    arrive(shared.at[pl.ds(0, nmode - 1)], FIRST)
-    sums_z(0, jnp.sum(shared[:, :, :size], axis=0))
     arrive(got.at[0, pl.ds(0, nmode - 1)], ENTRY)
     mix(0)
-    sums_y(0)
     arrive(hb.at[:, pl.ds(0, nz - 1), 0], FIELD_Z)
     push(hb.at[:, :, core], hb.at[:, :, core], FIELD_C, (mu, pair))
     pending.append((hb.at[:, :, 0], FIELD_C))
@@ -349,6 +350,9 @@
         if side:
             whole[1, :, om] = stage2[1, om]
 
+    spread(0)
+    sums_core(0)
+
     column = jnp.sum(weights[:, :1] * (ah[...].astype(F32) + al[...].astype(F32)), axis=0, keepdims=True)
     both = jnp.concatenate([own, column, jnp.zeros((6, modes), F32)], 0)
     products = jnp.dot(both, weights, precision=lax.Precision.HIGHEST, preferred_element_type=F32)
@@ -359,14 +363,11 @@
     arrive(hb.at[:, :, 0], FIELD_C)
     store_h(0, matrix(0), matrix(1))
 
-    spread(0)
-    sums_core(0)
+
+    spread_side(0)
     sums_y(1)
-
-    spread_side(0)
     spread_side(1)
     sums_x(1)
-
     source = sums_all(0)
     densities = [(matrix(2), matrix(3))]
     fields = tuple(matrix(part) for part in range(2))
@@ -397,7 +398,8 @@
 
     each(norb, send_result)
     pending.append((out.at[pl.ds(0, norb - 1)], RESULT))
-    out[om] = final[:, om]
+    keep = pltpu.make_async_copy(final.at[:, om], out.at[om], load.at[0])
+    keep.start()
 
     sums_core(1)
     chain = sums_all(1)
@@ -410,6 +412,7 @@
     for part in range(2):
         dout[part] = summed[part, pz, core]
 
+    keep.wait()
     arrive(out.at[pl.ds(0, norb - 1)], RESULT)
     for ref, index in pending:
         wait_for(ref, send.at[index])
@@ -430,7 +433,7 @@
                 jax.ShapeDtypeStruct(density.shape, F32),
             ),
             in_specs=[whole, whole, whole, pl.BlockSpec(memory_space=pltpu.SMEM), whole],
-            out_specs=(vmem, vmem),
+            out_specs=(whole, vmem),
             scratch_shapes=[
                 pltpu.VMEM((local, 2 * rows, size), F32),
                 pltpu.VMEM(density.shape, F32),

time: 82.2 us -> 80 us (0.973)
  Pallas kernels: 78.9 us -> 76.7 us
    pallas_call x1, Pallas kernels: 78.9 us -> 76.7 us  [on_device(): pl.pallas_call(functools.partial(kernel, (nx, ny, nz, rows, size)), out_s...]
where the time goes in v4:
time: 80 us; the launch traced here: 79.8 us
  Pallas kernels  76.7 us (96%)
  local copies, waits for them, and re-layouts  2.51 us (3%)
    pallas_call x1, Pallas kernels, on_device(): pl.pallas_call(functools.partial(kernel, (nx, ny, nz, rows, size)), out_s...  76.7 us
    unnamed x4, local copies, waits for them, and re-layouts  2.51 us

profile of v4, /device:TPU:1, one launch (start us, length us, event | category | flops | bytes accessed | tf_op | source)
XLA Modules:
  0.0 79.8 jit_solution(17960743675205505831)
XLA Ops:
  0.6 76.7 %shard_map.68 = (f32[16,2,16,256]{3,2,1,0:T(8,128)}, f32[2,16,256]{2,1,0:T(8,128)}) custom-call(f32[16,32,256]{2,1,0:T(8,128)} %bitcast.1, f32[2,16,256]{2,1,0:T(8,128)} %dens_hbm.1, f32[2,16,256]{2,1,0:T(8,128)} %bare_hbm.1, f32[16]{0:T(128)} %coup.1, f32[16,512]{1,0:T(8,128)} %prop_hbm.1), custom_call_target="tpu_custom_call" | custom-call | tf_op jit(solution)/shard_map/pallas_call | solution.py:429
  77.3 0.0 copy-start
  77.3 1.9 %copy.9 = f32[16,2,16,256]{3,2,1,0:T(8,128)} copy(f32[16,2,16,256]{3,2,1,0:T(8,128)} %get-tuple-element.4) | data formatting | bytes 1048576
  79.2 0.0 copy-done
  79.2 0.6 copy.10
Async XLA Ops:
  77.3 1.9 %copy-start = (f32[2,16,256]{2,1,0:T(8,128)S(1)}, f32[2,16,256]{2,1,0:T(8,128)}, u32[]{:S(2)}) copy-start(f32[2,16,256]{2,1,0:T(8,128)} %get-tuple-element.5) | copy-start | bytes 98308

commit v5 on v4

--- a/solution.py
+++ b/solution.py
@@ -50,7 +50,7 @@
     ENTRY, MIXED, WHOLE = base, base + 2, base + 4
     FIELD_Z, FIELD_C, RESULT, FIRST = base + 6, base + 7, base + 8, base + 9
     SUM_Z, SUM_Y, SUM_X, SUM_C = base + 10, base + 12, base + 14, base + 16
-    NEAR_MIXED, NEAR_WHOLE = base + 18, base + 19
+    NEAR_MIXED, NEAR_WHOLE = base + 18, base + 20
     mu, om = lax.axis_index("mode"), lax.axis_index("orb")
     px, py = mu // ny, mu % ny
     pz, core = om // CORES, om % CORES
@@ -272,31 +272,18 @@
             where = pl.ds(pl.multiple_of(first * span, span), span)
             mixed[h, where, :] = dot3((ah[where, :], al[where, :]), (high, low))
 
-            if h:
-                continue
-
-            def send_mixed(k, first=first):
-                nu = first * ny + (py + k) % ny
-                rows_of = pl.ds(pl.multiple_of(nu * norb, norb), norb)
-                push(mixed.at[h, rows_of], back.at[h, mu], MIXED, (nu, om))
-
-            if d:
-                send_mixed(0)
-            each(ny, send_mixed)
-        for side in range(2 * h):
+        for side in range(2):
             start = sides[side] * half
 
             def send_part(k):
                 nu = (mu + k) % nmode
                 rows_of = pl.ds(pl.multiple_of(nu * norb + start, half), half)
                 there = back.at[h, mu, pl.ds(pl.multiple_of(start, half), half)]
-                push(mixed.at[h, rows_of], there, (MIXED + 1, NEAR_MIXED)[side], (nu, om))
+                push(mixed.at[h, rows_of], there, (MIXED, NEAR_MIXED)[side] + h, (nu, om))
 
             each(nmode, send_part)
-            pending.append((back.at[h, pl.ds(0, nmode - 1), pl.ds(0, half)], (MIXED + 1, NEAR_MIXED)[side]))
+            pending.append((back.at[h, pl.ds(0, nmode - 1), pl.ds(0, half)], (MIXED, NEAR_MIXED)[side] + h))
         back[h, mu] = mixed[h, pl.ds(pl.multiple_of(mu * norb, norb), norb), :]
-        if h == 0:
-            pending.append((back.at[h, pl.ds(0, nmode - 1)], MIXED))
 
     arrive(got.at[0, pl.ds(0, nmode - 1)], ENTRY)
     mix(0)
@@ -319,38 +306,27 @@
         [jnp.sum(wide * mixed[h], axis=0, keepdims=True) for h in range(2)], 1
     ))
 
-    def spread(h):
-        arrive(back.at[h, pl.ds(0, nmode - 1)], MIXED + h)
-        stage2[h] = jnp.swapaxes(back[h], 0, 1).reshape(norb, 2, rows, cols)
-
-        def send_matrix(k):
-            target = (om + k) % norb
-            push(stage2.at[h, target], whole.at[h, :, om], WHOLE + h, (mu, target))
-
-        each(norb, send_matrix)
-        whole[h, :, om] = stage2[h, om]
-        pending.append((whole.at[h, :, pl.ds(0, norb - 1)], WHOLE + h))
-
-    def spread_side(side):
-        arrive(back.at[1, pl.ds(0, nmode - 1), pl.ds(0, half)], (MIXED + 1, NEAR_MIXED)[side])
+    def spread_side(h, side):
+        arrive(back.at[h, pl.ds(0, nmode - 1), pl.ds(0, half)], (MIXED, NEAR_MIXED)[side] + h)
         start = pl.multiple_of(sides[side] * half, half)
-        block = jnp.swapaxes(back[1, :, pl.ds(start, half), :], 0, 1)
-        stage2[1, pl.ds(start, half)] = block.reshape(half, 2, rows, cols)
-        index = (WHOLE + 1, NEAR_WHOLE)[side]
+        block = jnp.swapaxes(back[h, :, pl.ds(start, half), :], 0, 1)
+        stage2[h, pl.ds(start, half)] = block.reshape(half, 2, rows, cols)
+        index = (WHOLE, NEAR_WHOLE)[side] + h
 
         def send_matrix(k):
             target = start + (om + k) % half
-            push(stage2.at[1, target], whole.at[1, :, om], index, (mu, target))
+            push(stage2.at[h, target], whole.at[h, :, om], index, (mu, target))
 
         if side == 0:
             send_matrix(0)
         each(half, send_matrix)
         count = half - side
-        pending.append((whole.at[1, :, pl.ds(0, count)], index))
+        pending.append((whole.at[h, :, pl.ds(0, count)], index))
         if side:
-            whole[1, :, om] = stage2[1, om]
-
-    spread(0)
+            whole[h, :, om] = stage2[h, om]
+
+    spread_side(0, 0)
+    spread_side(0, 1)
     sums_core(0)
 
     column = jnp.sum(weights[:, :1] * (ah[...].astype(F32) + al[...].astype(F32)), axis=0, keepdims=True)
@@ -364,9 +340,9 @@
     store_h(0, matrix(0), matrix(1))
 
 
-    spread_side(0)
+    spread_side(1, 0)
     sums_y(1)
-    spread_side(1)
+    spread_side(1, 1)
     sums_x(1)
     source = sums_all(0)
     densities = [(matrix(2), matrix(3))]
@@ -378,9 +354,9 @@
         fields = tuple(fields[p] + (field_weight * time_step) * source[p] for p in range(2))
         store_h(step + 1, *fields)
 
-    arrive(whole.at[0, :, pl.ds(0, norb - 1)], WHOLE)
-    arrive(whole.at[1, :, pl.ds(0, half)], WHOLE + 1)
-    arrive(whole.at[1, :, pl.ds(0, half - 1)], NEAR_WHOLE)
+    for h in range(2):
+        arrive(whole.at[h, :, pl.ds(0, half)], WHOLE + h)
+        arrive(whole.at[h, :, pl.ds(0, half - 1)], NEAR_WHOLE + h)
     state = tuple(
         jnp.concatenate([whole[h, part].reshape(size, cols) for h in range(2)], 1)
         for part in range(2)
@@ -457,8 +433,8 @@
                 pltpu.VMEM((2, nz, CORES, rows, size), F32),
                 pltpu.VMEM((3, 2, 2 * size, 2 * size), BF16),
                 pltpu.VMEM((3, 2, 2 * size, 2 * size), BF16),
-                pltpu.SemaphoreType.DMA((2 * nx + 20,)),
-                pltpu.SemaphoreType.DMA((2 * nx + 20,)),
+                pltpu.SemaphoreType.DMA((2 * nx + 22,)),
+                pltpu.SemaphoreType.DMA((2 * nx + 22,)),
                 pltpu.SemaphoreType.DMA((4,)),
             ],
             compiler_params=pltpu.CompilerParams(

time: 80 us -> 78.7 us (0.984)
  Pallas kernels: 76.7 us -> 75.4 us
    pallas_call x1, Pallas kernels: 76.7 us -> 75.4 us  [on_device(): pl.pallas_call(functools.partial(kernel, (nx, ny, nz, rows, size)), out_s...]
where the time goes in v5:
time: 78.7 us; the launch traced here: 78.5 us
  Pallas kernels  75.4 us (96%)
  local copies, waits for them, and re-layouts  2.51 us (3%)
    pallas_call x1, Pallas kernels, on_device(): pl.pallas_call(functools.partial(kernel, (nx, ny, nz, rows, size)), out_s...  75.4 us
    unnamed x4, local copies, waits for them, and re-layouts  2.51 us

profile of v5, /device:TPU:1, one launch (start us, length us, event | category | flops | bytes accessed | tf_op | source)
XLA Modules:
  0.0 78.5 jit_solution(15218032798245675491)
XLA Ops:
  0.6 75.4 %shard_map.68 = (f32[16,2,16,256]{3,2,1,0:T(8,128)}, f32[2,16,256]{2,1,0:T(8,128)}) custom-call(f32[16,32,256]{2,1,0:T(8,128)} %bitcast.1, f32[2,16,256]{2,1,0:T(8,128)} %dens_hbm.1, f32[2,16,256]{2,1,0:T(8,128)} %bare_hbm.1, f32[16]{0:T(128)} %coup.1, f32[16,512]{1,0:T(8,128)} %prop_hbm.1), custom_call_target="tpu_custom_call" | custom-call | tf_op jit(solution)/shard_map/pallas_call | solution.py:405
  76.0 0.0 copy-start
  76.0 1.9 %copy.9 = f32[16,2,16,256]{3,2,1,0:T(8,128)} copy(f32[16,2,16,256]{3,2,1,0:T(8,128)} %get-tuple-element.4) | data formatting | bytes 1048576
  77.9 0.0 copy-done
  77.9 0.6 copy.10
Async XLA Ops:
  76.0 1.9 %copy-start = (f32[2,16,256]{2,1,0:T(8,128)S(1)}, f32[2,16,256]{2,1,0:T(8,128)}, u32[]{:S(2)}) copy-start(f32[2,16,256]{2,1,0:T(8,128)} %get-tuple-element.5) | copy-start | bytes 98308

commit v6 on v5

--- a/solution.py
+++ b/solution.py
@@ -325,9 +325,6 @@
         if side:
             whole[h, :, om] = stage2[h, om]
 
-    spread_side(0, 0)
-    spread_side(0, 1)
-    sums_core(0)
 
     column = jnp.sum(weights[:, :1] * (ah[...].astype(F32) + al[...].astype(F32)), axis=0, keepdims=True)
     both = jnp.concatenate([own, column, jnp.zeros((6, modes), F32)], 0)
@@ -338,6 +335,9 @@
     c_own = coup[om]
     arrive(hb.at[:, :, 0], FIELD_C)
     store_h(0, matrix(0), matrix(1))
+    spread_side(0, 0)
+    spread_side(0, 1)
+    sums_core(0)
 
 
     spread_side(1, 0)
@@ -361,18 +361,35 @@
         jnp.concatenate([whole[h, part].reshape(size, cols) for h in range(2)], 1)
         for part in range(2)
     )
-    for step in range(3):
-        weight = e_own if step < 2 else c_own
+    for step in range(2):
         state = turn(step, *state)
-        state = tuple(state[p] + (weight * time_step) * densities[step][p] for p in range(2))
+        state = tuple(state[p] + (e_own * time_step) * densities[step][p] for p in range(2))
     for part in range(2):
         final[part] = state[part].reshape(norb, rows, size)
-
-    def send_result(k):
-        target = (om + k) % norb
-        push(final.at[:, target], out.at[om], RESULT, (mu, target))
-
-    each(norb, send_result)
+        summed[part] = densities[2][part].reshape(nz, CORES, rows, size)
+    stacked = split(jnp.concatenate(state, 0))
+    span = half * rows
+    for side in range(2):
+        blocks = pl.ds(pl.multiple_of(sides[side] * half, half), half)
+        lines = pl.ds(pl.multiple_of(sides[side] * span, span), span)
+        lower = pl.ds(pl.multiple_of(size + sides[side] * span, span), span)
+        layers = pl.ds(sides[side] * (nz // 2), nz // 2)
+        own_rows = tuple(final[part, blocks].reshape(span, size) for part in range(2))
+        left = tuple(dot3((hl[2, 0, at, :], hl[2, 1, at, :]), stacked) for at in (lines, lower))
+        right = dot3(split(jnp.concatenate(own_rows, 1)), (hr[2, 0], hr[2, 1]))
+        change = (left[1] - right[:, size:], right[:, :size] - left[0])
+        for part in range(2):
+            value = own_rows[part] + change[part]
+            value = value + (c_own * time_step) * summed[part, layers].reshape(span, size)
+            final[part, blocks] = value.reshape(half, rows, size)
+
+        def send_result(k):
+            target = sides[side] * half + (om + k) % half
+            push(final.at[:, target], out.at[om], RESULT, (mu, target))
+
+        if side == 0:
+            send_result(0)
+        each(half, send_result)
     pending.append((out.at[pl.ds(0, norb - 1)], RESULT))
     keep = pltpu.make_async_copy(final.at[:, om], out.at[om], load.at[0])
     keep.start()

time: 78.7 us -> 78.4 us (level)
  no operation moved by 1% of the time
where the time goes in v6:
time: 78.4 us; the launch traced here: 78.3 us
  Pallas kernels  75.1 us (96%)
  local copies, waits for them, and re-layouts  2.51 us (3%)
    pallas_call x1, Pallas kernels, on_device(): pl.pallas_call(functools.partial(kernel, (nx, ny, nz, rows, size)), out_s...  75.1 us
    unnamed x4, local copies, waits for them, and re-layouts  2.51 us

profile of v6, /device:TPU:1, one launch (start us, length us, event | category | flops | bytes accessed | tf_op | source)
XLA Modules:
  0.0 78.3 jit_solution(11355260293145369550)
XLA Ops:
  0.6 75.1 %shard_map.68 = (f32[16,2,16,256]{3,2,1,0:T(8,128)}, f32[2,16,256]{2,1,0:T(8,128)}) custom-call(f32[16,32,256]{2,1,0:T(8,128)} %bitcast.1, f32[2,16,256]{2,1,0:T(8,128)} %dens_hbm.1, f32[2,16,256]{2,1,0:T(8,128)} %bare_hbm.1, f32[16]{0:T(128)} %coup.1, f32[16,512]{1,0:T(8,128)} %prop_hbm.1), custom_call_target="tpu_custom_call" | custom-call | tf_op jit(solution)/shard_map/pallas_call | solution.py:422
  75.7 0.0 copy-start
  75.8 1.9 %copy.9 = f32[16,2,16,256]{3,2,1,0:T(8,128)} copy(f32[16,2,16,256]{3,2,1,0:T(8,128)} %get-tuple-element.4) | data formatting | bytes 1048576
  77.6 0.0 copy-done
  77.6 0.6 copy.10
Async XLA Ops:
  75.7 1.9 %copy-start = (f32[2,16,256]{2,1,0:T(8,128)S(1)}, f32[2,16,256]{2,1,0:T(8,128)}, u32[]{:S(2)}) copy-start(f32[2,16,256]{2,1,0:T(8,128)} %get-tuple-element.5) | copy-start | bytes 98308
